TPU v7x, 32 devices: a whole 2x2x4 slice. The times are simulated.
32 devices in a mesh: tm: 4 (over y, x), row: 4 (over z), col: 2 (over core).
Axes of the slice: x: 2, y: 2, z: 4, core: 2. Of those that a mesh axis runs over, the one named last changes fastest.
Arguments:
- blocks: float32 [4, 4096, 4096], P('tm', 'row', 'col'), may hold values from -0.7 to 7.7, as said below
- borders: float32 [4, 640, 4096], P('tm', None, ('row', 'col')), may hold values from -0.3 to 0.3
- arrow_tip: float32 [128, 128], replicated, may hold values from -6 to 6
Outputs:
- schur_blocks: float32 [4, 4096, 4096], P('tm', 'row', 'col')
- factor_panels: float32 [4, 4096, 1024], P('tm', 'row')
- border_out: float32 [4, 640, 4096], P('tm', None, ('row', 'col'))
- tip_out: float32 [128, 128], replicated
Inputs may be any that keep to these rules, and one draw needn't show every extreme that they name: `blocks`: each partition's block is symmetric positive definite.
All inputs are finite; a program needn't handle non-finite values.
Results may differ from a plain program's by a relative error of at most 0.0001.
Values sent between devices are 32-bit elements; how exact they have to be, the bound alone decides.
A program may use at most 128 MiB of HBM per device.

v0:
```python
import jax
import jax.numpy as jnp
from jax import lax
from jax.sharding import PartitionSpec as P

F = 128
P_SIZE = 512
Q = 512
PANELS = 2


def from_behind(value, axis, steps):
    count = lax.axis_size(axis)
    first, last = (max(0, -steps), min(count, count - steps))
    return lax.ppermute(value, axis, [(source, source + steps) for source in range(first, last)])


def exact_dot(left, right):
    return jnp.dot(left, right, precision=lax.Precision.HIGHEST, preferred_element_type=jnp.float32)


def right_solve(chol, values):
    return lax.linalg.triangular_solve(chol, values, left_side=False, lower=True, transpose_a=True)


def shards(blocks, borders, arrow_tip):
    block = blocks[0]
    border = borders[0]
    n_row = lax.axis_size("row")
    n_col = lax.axis_size("col")
    row_id = lax.axis_index("row")
    col_id = lax.axis_index("col")
    rows_dev, cols_dev = block.shape
    border_rows, width = border.shape
    piece = P_SIZE // n_row
    per_col = n_row // n_col
    half = rows_dev // n_col
    node_block = row_id * n_col + col_id
    target = jnp.logical_and(row_id == n_row - 1, col_id == n_col - 1).astype(jnp.float32)
    tip_term = jnp.zeros((F, F), jnp.float32)
    factors = []
    for k in range(PANELS):
        column_parts = [
            block[:, j * rows_dev + k * piece : j * rows_dev + (k + 1) * piece]
            for j in range(per_col)
        ]
        local_panel = jnp.concatenate(column_parts, axis=1)
        panel = lax.all_gather(local_panel, "col", axis=1, tiled=True)
        corner = lax.all_gather(panel[k * piece : (k + 1) * piece], "row", axis=0, tiled=True)
        chol = jnp.linalg.cholesky(corner)
        start = col_id * half
        mine = lax.dynamic_slice_in_dim(panel, start, half, 0)
        offsets = start + jnp.arange(half, dtype=jnp.int32)
        part = right_solve(chol, mine)
        part = jnp.where((offsets < k * piece)[:, None], jnp.float32(0.0), part)
        every = lax.all_gather(part, ("row", "col"), axis=0, tiled=True)
        factor = lax.dynamic_slice_in_dim(every, row_id * rows_dev, rows_dev, 0)
        columns = lax.dynamic_slice_in_dim(every, col_id * cols_dev, cols_dev, 0)
        own_nodes = lax.dynamic_slice_in_dim(every, node_block * width, width, 0)
        edge = lax.all_gather(
            border[:, k * piece : (k + 1) * piece], ("row", "col"), axis=1, tiled=True
        )
        edge = edge.reshape(border_rows, n_row, n_col, piece)[:, :, 0, :].reshape(
            border_rows, P_SIZE
        )
        arrow = right_solve(chol, edge)
        block = block - exact_dot(factor, columns.T)
        border = border - exact_dot(arrow, own_nodes.T)
        step_handoff = exact_dot(arrow, arrow[:Q].T)
        step_tip = exact_dot(arrow[Q:], arrow[Q:].T)
        factors.append(factor)
        incoming = from_behind(step_handoff, "tm", 1)
        receive_block = block
        receive_border = border
        receive_block = receive_block.at[rows_dev - Q :, cols_dev - Q :].add(-target * incoming[:Q])
        receive_border = receive_border.at[Q:, width - Q :].add(-target * incoming[Q:])
        block = receive_block
        border = receive_border
        tip_term = tip_term + lax.psum(step_tip, "tm")
    tip_out = arrow_tip - tip_term
    return (block[None], jnp.concatenate(factors, axis=1)[None], border[None], tip_out)


def solution(mesh):
    placed = (P("tm", "row", "col"), P("tm", None, ("row", "col")), P())
    return jax.shard_map(
        shards,
        mesh=mesh,
        in_specs=placed,
        out_specs=(P("tm", "row", "col"), P("tm", "row", None), P("tm", None, ("row", "col")), P()),
        check_vma=False,
    )
```

profile of v0, /device:TPU:0, one launch (start us, length us, event | category | flops | bytes accessed | tf_op | source)
XLA Modules:
  0.0 700.4 jit_solution(12227775118571190045)
XLA Ops:
  18.9 13.4 %all-gather.9.cloned.1.call-done = f32[1024,512]{0,1:T(8,128)} async-done(((f32[1024,256]{0,1:T(8,128)}), f32[1024,512]{0,1:T(8,128)}) %all-gather.9.cloned.1.call-update) | async-done | bytes 2097168 | tf_op jit(solution)/shard_map/all_gather | solution.py:48
  35.3 30.5 %all-gather.11.cloned.1.call-done = f32[512,512]{0,1:T(8,128)} async-done(((f32[128,512]{0,1:T(8,128)}), f32[512,512]{0,1:T(8,128)}) %all-gather.11.cloned.1.call-update) | async-done | bytes 1048592 | tf_op jit(solution)/shard_map/all_gather | solution.py:49
  68.7 11.7 %cholesky.286 = f32[128,128]{1,0:T(8,128)S(1)} custom-call(f32[128,128]{1,0:T(8,128)S(1)} %cholesky.426), custom_call_target="Cholesky" | custom-call | tf_op jit(solution)/shard_map/jit(cholesky)/cholesky | solution.py:50
  80.4 9.8 %custom-call.31 = f32[1,128,128]{1,2,0:T(8,128)S(1)} custom-call(f32[1,128,128]{2,1,0:T(8,128)S(1)} %get-tuple-element.134), custom_call_target="InvertDiagBlocksLowerTriangular" | custom-call | tf_op jit(solution)/shard_map/jit(cholesky)/cholesky | solution.py:50
  91.0 11.7 %cholesky.305 = f32[128,128]{1,0:T(8,128)S(1)} custom-call(f32[128,128]{1,0:T(8,128)S(1)} %cholesky.430), custom_call_target="Cholesky" | custom-call | tf_op jit(solution)/shard_map/jit(cholesky)/cholesky | solution.py:50
  102.8 10.1 %custom-call.32 = f32[1,128,128]{1,2,0:T(8,128)S(1)} custom-call(f32[1,128,128]{2,1,0:T(8,128)S(1)} %get-tuple-element.131), custom_call_target="InvertDiagBlocksLowerTriangular" | custom-call | tf_op jit(solution)/shard_map/jit(cholesky)/cholesky | solution.py:50
  113.6 11.7 %cholesky.326 = f32[128,128]{1,0:T(8,128)S(1)} custom-call(f32[128,128]{1,0:T(8,128)S(1)} %cholesky.435), custom_call_target="Cholesky" | custom-call | tf_op jit(solution)/shard_map/jit(cholesky)/cholesky | solution.py:50
  125.3 9.8 %custom-call.33 = f32[1,128,128]{1,2,0:T(8,128)S(1)} custom-call(f32[1,128,128]{2,1,0:T(8,128)S(1)} %get-tuple-element.128), custom_call_target="InvertDiagBlocksLowerTriangular" | custom-call | tf_op jit(solution)/shard_map/jit(cholesky)/cholesky | solution.py:50
  135.8 11.7 %cholesky.343 = f32[128,128]{1,0:T(8,128)S(1)} custom-call(f32[128,128]{1,0:T(8,128)S(1)} %convolution_subtract_fusion.19), custom_call_target="Cholesky" | custom-call | tf_op jit(solution)/shard_map/jit(cholesky)/cholesky | solution.py:50
  160.3 39.3 %custom-call.34 = f32[4,128,128]{1,2,0:T(8,128)S(1)} custom-call(f32[4,128,128]{2,1,0:T(8,128)S(1)} %get-tuple-element.83), custom_call_target="InvertDiagBlocksLowerTriangular" | custom-call | tf_op jit(solution)/shard_map/triangular_solve/custom-call.3 | solution.py:23
  220.8 67.5 %all-gather.13.cloned.1.call-done = f32[4096,512]{0,1:T(8,128)} async-done(((f32[512,512]{0,1:T(8,128)}), f32[4096,512]{0,1:T(8,128)}) %all-gather.13.cloned.1.call-update) | async-done | bytes 8388624 | tf_op jit(solution)/shard_map/all_gather | solution.py:56
  290.0 16.3 %fusion.4 = f32[1024,2048]{0,1:T(8,128)S(1)} fusion(f32[1024,512]{0,1:T(8,128)S(1)} %constant_dynamic-slice_fusion.3, f32[4096,512]{0,1:T(8,128)} %all-gather.13.cloned.1.call-done, s32[]{:T(128)S(6)} %select_n.29, f32[1,1024,2048]{1,2,0:T(8,128)} %copy.7), kind=kOutput, calls=%fused_computation.9 | convolution fusion | flops 12886999040 | bytes 23068676 | tf_op jit(solution)/shard_map/dot_general | solution.py:19
  332.3 22.9 %all-gather.19.cloned.1.call-done = f32[512,512]{0,1:T(8,128)} async-done(((f32[128,512]{0,1:T(8,128)}), f32[512,512]{0,1:T(8,128)}) %all-gather.19.cloned.1.call-update) | async-done | bytes 1048592 | tf_op jit(solution)/shard_map/all_gather | solution.py:49
  360.2 11.7 %cholesky.358 = f32[128,128]{1,0:T(8,128)S(1)} custom-call(f32[128,128]{1,0:T(8,128)S(1)} %cholesky.439), custom_call_target="Cholesky" | custom-call | tf_op jit(solution)/shard_map/jit(cholesky)/cholesky | solution.py:50
  384.4 11.7 %cholesky.377 = f32[128,128]{1,0:T(8,128)S(1)} custom-call(f32[128,128]{1,0:T(8,128)S(1)} %cholesky.443), custom_call_target="Cholesky" | custom-call | tf_op jit(solution)/shard_map/jit(cholesky)/cholesky | solution.py:50
  396.2 10.0 %custom-call.37 = f32[1,128,128]{1,2,0:T(8,128)S(1)} custom-call(f32[1,128,128]{2,1,0:T(8,128)S(1)} %get-tuple-element.121), custom_call_target="InvertDiagBlocksLowerTriangular" | custom-call | tf_op jit(solution)/shard_map/jit(cholesky)/cholesky | solution.py:50
  407.7 11.7 %cholesky.398 = f32[128,128]{1,0:T(8,128)S(1)} custom-call(f32[128,128]{1,0:T(8,128)S(1)} %cholesky.448), custom_call_target="Cholesky" | custom-call | tf_op jit(solution)/shard_map/jit(cholesky)/cholesky | solution.py:50
  419.4 9.8 %custom-call.38 = f32[1,128,128]{1,2,0:T(8,128)S(1)} custom-call(f32[1,128,128]{2,1,0:T(8,128)S(1)} %get-tuple-element.118), custom_call_target="InvertDiagBlocksLowerTriangular" | custom-call | tf_op jit(solution)/shard_map/jit(cholesky)/cholesky | solution.py:50
  430.7 11.7 %cholesky.415 = f32[128,128]{1,0:T(8,128)S(1)} custom-call(f32[128,128]{1,0:T(8,128)S(1)} %convolution_subtract_fusion.18), custom_call_target="Cholesky" | custom-call | tf_op jit(solution)/shard_map/jit(cholesky)/cholesky | solution.py:50
  448.9 11.8 %while.13 = (s32[]{:T(128)}, f32[512,512]{1,0:T(8,128)}, s32[4,2]{0,1:T(2,128)S(1)}, f32[4,128,128]{2,1,0:T(8,128)S(1)}, s32[]{:T(128)}) while((s32[]{:T(128)}, f32[512,512]{1,0:T(8,128)}, s32[4,2]{0,1:T(2,128)S(1)}, f32[4,128,128]{2,1,0:T(8,128)S(1)}, s32[]{:T(128)}) %tuple.106), condition=%wide.while_cond.4.clone, body=%wide.while_body.4.clone.sunk | while | flops 2 | bytes 131189 | solution.py:23
  460.7 39.3 %custom-call.39 = f32[4,128,128]{1,2,0:T(8,128)S(1)} custom-call(f32[4,128,128]{2,1,0:T(8,128)S(1)} %get-tuple-element.85), custom_call_target="InvertDiagBlocksLowerTriangular" | custom-call | tf_op jit(solution)/shard_map/triangular_solve/custom-call.3 | solution.py:23
  531.0 29.3 %all-reduce.3.cloned.1.call-done = f32[128,128]{1,0:T(8,128)} async-done(((f32[128,128]{1,0:T(8,128)}), f32[128,128]{1,0:T(8,128)}) %all-reduce.3.cloned.1.call-update) | async-done | bytes 65552 | tf_op jit(solution)/shard_map/psum | solution.py:79
  561.7 82.2 %all-gather.21.cloned.1.call-done = f32[4096,512]{0,1:T(8,128)} async-done(((f32[512,512]{0,1:T(8,128)}), f32[4096,512]{0,1:T(8,128)}) %all-gather.21.cloned.1.call-update) | async-done | bytes 8388624 | tf_op jit(solution)/shard_map/all_gather | solution.py:56
  661.9 16.6 %fusion.7 = f32[1024,2048]{0,1:T(8,128)S(1)} fusion(f32[1024,2048]{0,1:T(8,128)} %copy-done, f32[1024,512]{0,1:T(8,128)S(1)} %copy-done.2, f32[4096,512]{0,1:T(8,128)} %all-gather.21.cloned.1.call-done, s32[]{:T(128)S(6)} %select_n.29), kind=kOutput, calls=%fused_computation.10 | convolution fusion | flops 12886999040 | bytes 23068676 | tf_op jit(solution)/shard_map/dot_general | solution.py:19
  (199 shorter events, 187.5 us)
Async XLA Ops:
  7.2 25.1 %all-gather.9.cloned.1.call-start = ((), (), s32[]{:S(2)}) async-start(), calls=%async_computation | async-start | bytes 3145728 | tf_op jit(solution)/shard_map/all_gather | solution.py:48
  18.8 15.2 %copy-start.15 = (f32[1,640,512]{2,1,0:T(8,128)S(1)}, f32[1,640,512]{2,1,0:T(8,128)}, u32[]{:S(2)}) copy-start(f32[1,640,512]{2,1,0:T(8,128)} %param.17) | copy-start | bytes 3932164
  18.8 47.0 %all-gather.11.cloned.1.call-start = ((), (), s32[]{:S(2)}) async-start(), calls=%async_computation.1 | async-start | bytes 1310720 | tf_op jit(solution)/shard_map/all_gather | solution.py:49
  33.9 173.9 %all-gather.15.cloned.1.call-start = ((), (), s32[]{:S(2)}) async-start(), calls=%async_computation.3 | async-start | bytes 2949120 | tf_op jit(solution)/shard_map/all_gather | solution.py:60
  34.4 33.0 %copy-start.4 = (f32[1,640,512]{1,2,0:T(8,128)}, f32[1,640,512]{1,2,0:T(8,128)S(1)}, u32[]{:S(2)}) copy-start(f32[1,640,512]{1,2,0:T(8,128)S(1)} %copy.10) | copy-start | bytes 3932164
  35.2 253.1 %all-gather.13.cloned.1.call-start = ((), (), s32[]{:S(2)}) async-start(), calls=%async_computation.2 | async-start | bytes 9437184 | tf_op jit(solution)/shard_map/all_gather | solution.py:56
  65.8 1.7 copy-start.9
  68.7 21.7 %copy-start.12 = (f32[512,512]{1,0:T(8,128)S(1)}, f32[512,512]{1,0:T(8,128)}, u32[]{:S(2)}) copy-start(f32[512,512]{1,0:T(8,128)} %copy-done.11) | copy-start | bytes 3145732
  207.8 114.0 %all-gather.17.cloned.1.call-start = ((), (), s32[]{:S(2)}) async-start(), calls=%async_computation.4 | async-start | bytes 3145728 | tf_op jit(solution)/shard_map/all_gather | solution.py:48
  217.1 89.2 %collective-permute-start = (f32[640,512]{0,1:T(8,128)}, f32[640,512]{0,1:T(8,128)}, u32[]{:S(2)}, u32[]{:S(2)}) collective-permute-start(f32[640,512]{0,1:T(8,128)} %fusion.17), channel_id=1, source_target_pairs={{0,8},{8,16},{16,24},{1,9},{9,17},{17,25},{2,10},{10,18},{18,26},{... | collective-permute-start | bytes 3932168 | tf_op jit(solution)/shard_map/ppermute | solution.py:15
  307.9 3.4 copy-start
  312.5 42.6 %all-gather.19.cloned.1.call-start = ((), (), s32[]{:S(2)}) async-start(), calls=%async_computation.5 | async-start | bytes 1310720 | tf_op jit(solution)/shard_map/all_gather | solution.py:49
  323.4 186.5 %all-gather.23.cloned.1.call-start = ((), (), s32[]{:S(2)}) async-start(), calls=%async_computation.7 | async-start | bytes 2949120 | tf_op jit(solution)/shard_map/all_gather | solution.py:60
  331.8 228.4 %all-reduce.3.cloned.1.call-start = ((), (), s32[]{:S(2)}) async-start(), calls=%async_computation.8 | async-start | bytes 131072 | tf_op jit(solution)/shard_map/psum | solution.py:79
  355.1 2.6 copy-start.8
  500.0 3.3 copy-start.16
  503.3 4.6 copy-start.10
  506.1 5.3 copy-start.14
  509.9 1.5 copy-start.17
  519.9 124.0 %all-gather.21.cloned.1.call-start = ((), (), s32[]{:S(2)}) async-start(), calls=%async_computation.6 | async-start | bytes 9437184 | tf_op jit(solution)/shard_map/all_gather | solution.py:56
  523.5 36.7 %copy-start.18 = (f32[128,128]{1,0:T(8,128)S(1)}, f32[128,128]{1,0:T(8,128)}, u32[]{:S(2)}) copy-start(f32[128,128]{1,0:T(8,128)} %param.18) | copy-start | bytes 196612
  523.5 120.3 %copy-start.7 = (f32[640,128]{0,1:T(8,128)S(1)}, f32[640,128]{0,1:T(8,128)}, u32[]{:S(2)}) copy-start(f32[640,128]{0,1:T(8,128)} %copy-done.6) | copy-start | bytes 983044
  527.5 121.0 %collective-permute-start.1 = (f32[640,512]{0,1:T(8,128)}, f32[640,512]{0,1:T(8,128)}, u32[]{:S(2)}, u32[]{:S(2)}) collective-permute-start(f32[640,512]{0,1:T(8,128)} %fusion.13), channel_id=1, source_target_pairs={{0,8},{8,16},{16,24},{1,9},{9,17},{17,25},{2,10},{10,18},{18,26},{... | collective-permute-start | bytes 3932168 | tf_op jit(solution)/shard_map/ppermute | solution.py:15
  656.4 5.5 copy-start.2
  (6 other events, 6.4 us)
Sparse Core Ops, SparseCore 0:
  18.9 13.2 all-gather.8
  34.4 31.3 all-gather.10
  67.4 32.3 all-gather.14
  207.9 80.3 all-gather.12
  312.6 9.0 all-gather.16
  323.7 31.3 all-gather.18
  356.8 32.1 all-gather.22
  520.0 40.2 all-reduce.2
  561.9 81.8 all-gather.20
where the time goes:
time: 712 us; the launch traced here: 700 us
  other arithmetic  256 us (36%)
  waiting for transfers between devices  255 us (36%)
  matrix products  85.7 us (12%)
  local copies, waits for them, and re-layouts  75 us (11%)
  between operations  20.2 us (3%)
  starting transfers between devices  8.1 us (1%)
    another operation x29, other arithmetic, shards(): chol = jnp.linalg.cholesky(corner)  158 us
    all_gather x2, waiting for transfers between devices, shards(): every = lax.all_gather(part, ('row', 'col'), axis=0, tiled=True)  150 us
    another operation x7, other arithmetic, right_solve(): lax.linalg.triangular_solve(chol, values, left_side=False, lower=True, tr...  81.4 us
    all_gather x2, waiting for transfers between devices, shards(): lax.all_gather(panel[k * piece:(k + 1) * piece], 'row', axis=0, tiled=True)  53.3 us
    dot_general x8, matrix products, exact_dot(): jnp.dot(left, right, precision=lax.Precision.HIGHEST, preferred_element_t...  51.4 us
    unnamed x45, local copies, waits for them, and re-layouts  38.2 us
    psum x1, waiting for transfers between devices, shards(): tip_term = tip_term + lax.psum(step_tip, 'tm')  29.3 us
    another operation x28, matrix products, right_solve(): lax.linalg.triangular_solve(chol, values, left_side=False, lower=True, tr...  27 us
  transfers between devices with their start and end apart: 11, of which 7 were waited for; matrix products, arithmetic and copies ran while one was open for 48% of the time, Pallas kernels for 0%

commit v1 on v0

v1 whole, which is shorter than its diff:
```python
import jax
import jax.numpy as jnp
from jax import lax
from jax.experimental import pallas as pl
from jax.experimental.pallas import tpu as pltpu
from jax.sharding import PartitionSpec as P

F = 128
P_SIZE = 512
Q = 512
PANELS = 2
BLOCK = 128
TILE = 16


def mm(left, right, precision=lax.Precision.HIGH):
    return jnp.dot(left, right, precision=precision, preferred_element_type=jnp.float32)


def dot_full(left, right):
    return lax.dot_general(
        left, right, (((1,), (0,)), ((), ())),
        precision=lax.Precision.HIGHEST, preferred_element_type=jnp.float32,
    )


def dot_first(left, right):
    return lax.dot_general(
        left, right, (((0,), (0,)), ((), ())),
        precision=lax.Precision.HIGHEST, preferred_element_type=jnp.float32,
    )


def inverse_factor_kernel(corner_ref, out_ref, work, pair):
    size = corner_ref.shape[0]
    work[...] = corner_ref[...]
    out_ref[...] = jnp.zeros_like(out_ref)
    row_of = lax.broadcasted_iota(jnp.int32, (BLOCK, BLOCK), 0)
    col_of = lax.broadcasted_iota(jnp.int32, (BLOCK, BLOCK), 1)
    eye = (row_of == col_of).astype(jnp.float32)
    sub = lax.broadcasted_iota(jnp.int32, (TILE, BLOCK), 0)
    deep = lax.broadcasted_iota(jnp.int32, (BLOCK, 2 * BLOCK), 0)

    def tile_step(t, carry):
        start = pl.multiple_of(t * TILE, TILE)
        left = pair[pl.ds(start, TILE), :BLOCK]
        right = pair[pl.ds(start, TILE), BLOCK:]
        turned = pltpu.roll(left, BLOCK - start, axis=1)
        lanes = [jnp.broadcast_to(turned[:, s : s + 1], (TILE, BLOCK)) for s in range(TILE)]
        for s in range(TILE):
            scale = lax.rsqrt(lanes[s][s : s + 1, :])
            coef = jnp.where(sub > s, lanes[s] * scale, 0.0)
            row_l = left[s : s + 1, :] * scale
            row_r = right[s : s + 1, :] * scale
            for u in range(s + 1, TILE):
                lanes[u] = lanes[u] - coef * (lanes[u][s : s + 1, :] * scale)
            left = jnp.where(sub == s, row_l, left - coef * row_l)
            right = jnp.where(sub == s, row_r, right - coef * row_r)
        pair[pl.ds(start, TILE), :BLOCK] = left
        pair[pl.ds(start, TILE), BLOCK:] = right
        both = jnp.concatenate([left, right], axis=1)
        change = dot_first(left, both)
        pair[...] = pair[...] - jnp.where(deep >= start + TILE, change, 0.0)
        return carry

    for b in range(size // BLOCK):
        lo, hi = b * BLOCK, (b + 1) * BLOCK
        pair[:, :BLOCK] = work[lo:hi, lo:hi]
        pair[:, BLOCK:] = eye
        lax.fori_loop(0, BLOCK // TILE, tile_step, 0)
        inv = pair[:, BLOCK:]
        if lo:
            done = dot_full(inv, out_ref[lo:hi, :lo])
            out_ref[lo:hi, :lo] = done
        out_ref[lo:hi, lo:hi] = inv
        if hi < size:
            across = dot_full(inv, work[lo:hi, hi:])
            work[hi:, hi:] = work[hi:, hi:] - dot_first(across, across)
            out_ref[hi:, :hi] = out_ref[hi:, :hi] - dot_first(across, out_ref[lo:hi, :hi])


def inverse_factor(corner):
    size = corner.shape[0]
    return pl.pallas_call(
        inverse_factor_kernel,
        out_shape=jax.ShapeDtypeStruct(corner.shape, jnp.float32),
        in_specs=[pl.BlockSpec(memory_space=pltpu.VMEM)],
        out_specs=pl.BlockSpec(memory_space=pltpu.VMEM),
        scratch_shapes=[
            pltpu.VMEM((size, size), jnp.float32),
            pltpu.VMEM((BLOCK, 2 * BLOCK), jnp.float32),
        ],
        cost_estimate=pl.CostEstimate(
            flops=60000 * size * size // 8, bytes_accessed=8 * size * size, transcendentals=size
        ),
        compiler_params=pltpu.CompilerParams(vmem_limit_bytes=24 * 1024 * 1024),
    )(corner)


def shards(blocks, borders, arrow_tip):
    block = blocks[0]
    border = borders[0]
    n_tm = lax.axis_size("tm")
    n_row = lax.axis_size("row")
    n_col = lax.axis_size("col")
    row_id = lax.axis_index("row")
    col_id = lax.axis_index("col")
    rows_dev, cols_dev = block.shape
    border_rows, width = border.shape
    piece = P_SIZE // n_row
    per_col = n_row // n_col
    target = jnp.logical_and(row_id == n_row - 1, col_id == n_col - 1)

    def panel_columns(rows, k):
        return jnp.concatenate(
            [
                rows[:, j * rows_dev + k * piece : j * rows_dev + (k + 1) * piece]
                for j in range(per_col)
            ],
            axis=1,
        )

    corners = []
    for k in range(PANELS):
        mine = block[k * piece : (k + 1) * piece]
        mine = jnp.concatenate([panel_columns(mine, i) for i in range(k + 1)], axis=1)
        every = lax.all_gather(mine, ("row", "col"), axis=0, tiled=False)
        every = every.reshape(n_row, n_col, piece, k + 1, per_col * piece)
        every = jnp.transpose(every, (3, 0, 2, 1, 4)).reshape(k + 1, P_SIZE, P_SIZE)
        corners.append(every)

    sides = [
        lax.all_gather(panel_columns(block, k), "col", axis=1, tiled=True) for k in range(PANELS)
    ]
    tops = [
        lax.all_gather(block[k * piece : (k + 1) * piece], "row", axis=0, tiled=True)
        for k in range(PANELS)
    ]
    share = border_rows // n_col
    held = border[:, : PANELS * piece]
    part = held[:share]
    for c in range(1, n_col):
        sent = lax.ppermute(held[c * share : (c + 1) * share], "col", [(0, c)])
        part = jnp.where(col_id == c, sent, part)
    edges = lax.all_gather(part, ("row", "col"), axis=0, tiled=False)
    edges = edges.reshape(n_row, n_col, share, PANELS, piece)
    edges = jnp.transpose(edges, (3, 1, 2, 0, 4)).reshape(PANELS, border_rows, P_SIZE)

    inverses = []
    below = [[None] * PANELS for _ in range(PANELS)]
    for k in range(PANELS):
        corner = corners[k][k]
        for i in range(k):
            left = corners[k][i]
            for j in range(i):
                left = left - mm(below[k][j], below[i][j].T, lax.Precision.HIGHEST)
            below[k][i] = mm(left, inverses[i].T, lax.Precision.HIGHEST)
            corner = corner - mm(below[k][i], below[k][i].T, lax.Precision.HIGHEST)
        inverses.append(inverse_factor(corner))

    arrows, rows, columns = [], [], []
    for k in range(PANELS):
        edge = edges[k]
        for i in range(k):
            edge = edge - mm(arrows[i], below[k][i].T)
        arrows.append(mm(edge, inverses[k].T))
    arrow = jnp.concatenate(arrows, axis=1)
    handoff = mm(arrow, arrow[:Q].T)
    tip = mm(arrow[Q:], arrow[Q:].T)
    incoming = lax.ppermute(handoff, "tm", [(t, t + 1) for t in range(n_tm - 1)])
    tip_out = arrow_tip - lax.psum(tip, "tm")

    node = jnp.arange(rows_dev, dtype=jnp.int32)
    node_col = jnp.arange(cols_dev, dtype=jnp.int32) % rows_dev
    for k in range(PANELS):
        side, top = sides[k], tops[k]
        for i in range(k):
            side = side - mm(rows[i], below[k][i].T)
            top = top - mm(below[k][i], columns[i])
        side = mm(side, inverses[k].T)
        top = mm(inverses[k], top)
        if k:
            side = jnp.where((node < k * piece)[:, None], jnp.float32(0.0), side)
            top = jnp.where((node_col < k * piece)[None, :], jnp.float32(0.0), top)
        rows.append(side)
        columns.append(top)
    factor = jnp.concatenate(rows, axis=1)
    own = lax.dynamic_slice_in_dim(factor, col_id * width, width, 0)
    block = block - mm(factor, jnp.concatenate(columns, axis=0))
    border = border - mm(arrow, own.T)
    taken = jnp.where(target, incoming, jnp.float32(0.0))
    block = block.at[rows_dev - Q :, cols_dev - Q :].add(-taken[:Q])
    border = border.at[Q:, width - Q :].add(-taken[Q:])
    return (block[None], factor[None], border[None], tip_out)


def solution(mesh):
    placed = (P("tm", "row", "col"), P("tm", None, ("row", "col")), P())
    return jax.shard_map(
        shards,
        mesh=mesh,
        in_specs=placed,
        out_specs=(P("tm", "row", "col"), P("tm", "row", None), P("tm", None, ("row", "col")), P()),
        check_vma=False,
    )
```

time: 712 us -> 382 us (0.54); the launches traced: 700 us -> 379 us
  other arithmetic: 256 us -> 11.5 us
  waiting for transfers between devices: 255 us -> 184 us
  Pallas kernels: 0 us -> 49.4 us
  local copies, waits for them, and re-layouts: 75 us -> 42.5 us
  matrix products: 85.7 us -> 69.3 us
    another operation x36 -> x0, other arithmetic: 239 us -> none  [the longest x29 158 us: shards(): chol = jnp.linalg.cholesky(corner)]
    all_gather x8 -> x7, waiting for transfers between devices: 226 us -> 168 us  [the longest x2 146 us: shards(): lax.all_gather(block[k * piece:(k + 1) * piece], 'row', axis=0, tiled=True)]
    pallas_call x0 -> x2, Pallas kernels: none -> 49.4 us  [inverse_factor(): pl.pallas_call(inverse_factor_kernel, out_shape=jax.ShapeDtypeStruct(corn...]
    another operation x40 -> x0, matrix products: 34.3 us -> none  [the longest x28 27 us: right_solve(): lax.linalg.triangular_solve(chol, values, left_side=False, lower=True, tr...]
    another operation x35 -> x0, local copies, waits for them, and re-layouts: 19.9 us -> none  [the longest x27 19.6 us: right_solve(): lax.linalg.triangular_solve(chol, values, left_side=False, lower=True, tr...]
    dot_general x8 -> x15, matrix products: 51.4 us -> 69.3 us  [mm(): jnp.dot(left, right, precision=precision, preferred_element_type=jnp.floa...]
    unnamed x45 -> x42, local copies, waits for them, and re-layouts: 38.2 us -> 22.7 us
    psum x1, waiting for transfers between devices: 29.3 us -> 14.5 us  [shards(): tip_out = arrow_tip - lax.psum(tip, 'tm')]
  transfers between devices with their start and end apart: 11 -> 10, of which waited for: 7 -> 7; matrix products, arithmetic and copies ran while one was open for 48% -> 20% of each run, Pallas kernels for 0% -> 13%
where the time goes in v1:
time: 382 us; the launch traced here: 379 us
  waiting for transfers between devices  184 us (48%)
  matrix products  69.3 us (18%)
  Pallas kernels  49.4 us (13%)
  local copies, waits for them, and re-layouts  42.5 us (11%)
  between operations  14.7 us (4%)
  other arithmetic  11.5 us (3%)
  starting transfers between devices  7.51 us (2%)
    all_gather x2, waiting for transfers between devices, shards(): lax.all_gather(block[k * piece:(k + 1) * piece], 'row', axis=0, tiled=True)  146 us
    dot_general x15, matrix products, mm(): jnp.dot(left, right, precision=precision, preferred_element_type=jnp.floa...  69.3 us
    pallas_call x2, Pallas kernels, inverse_factor(): pl.pallas_call(inverse_factor_kernel, out_shape=jax.ShapeDtypeStruct(corn...  49.4 us
    unnamed x42, local copies, waits for them, and re-layouts  22.7 us
    all_gather x2, waiting for transfers between devices, shards(): every = lax.all_gather(mine, ('row', 'col'), axis=0, tiled=False)  20 us
    psum x1, waiting for transfers between devices, shards(): tip_out = arrow_tip - lax.psum(tip, 'tm')  14.5 us
    reshape x2, local copies, waits for them, and re-layouts, shards(): edges = edges.reshape(n_row, n_col, share, PANELS, piece)  7.67 us
  transfers between devices with their start and end apart: 10, of which 7 were waited for; matrix products, arithmetic and copies ran while one was open for 20% of the time, Pallas kernels for 13%

profile of v1, /device:TPU:0, one launch (start us, length us, event | category | flops | bytes accessed | tf_op | source)
XLA Modules:
  0.0 379.3 jit_solution(7743753361952217652)
XLA Ops:
  7.2 3.3 fusion.48
  20.5 15.7 %all-gather.17.cloned.1.call-done = f32[1024,256]{1,0:T(8,128)} async-done(((f32[128,256]{1,0:T(8,128)}), f32[1024,256]{1,0:T(8,128)}) %all-gather.17.cloned.1.call-update) | async-done | bytes 1048592 | tf_op jit(solution)/shard_map/all_gather | solution.py:127
  38.3 24.7 %shard_map.66 = f32[512,512]{1,0:T(8,128)S(1)} custom-call(f32[512,512]{1,0:T(8,128)S(1)} %bitcast.72), custom_call_target="tpu_custom_call" | custom-call | flops 1966080000 | bytes 2097152 | tf_op jit(solution)/shard_map/pallas_call | solution.py:84
  63.0 4.3 %all-gather.19.cloned.1.call-done = f32[1024,512]{1,0:T(8,128)} async-done(((f32[128,512]{1,0:T(8,128)}), f32[1024,512]{1,0:T(8,128)}) %all-gather.19.cloned.1.call-update) | async-done | bytes 2097168 | tf_op jit(solution)/shard_map/all_gather | solution.py:127
  67.4 2.6 reshape.105
  77.2 24.7 %shard_map.67 = f32[512,512]{1,0:T(8,128)S(1)} custom-call(f32[512,512]{1,0:T(8,128)S(1)} %convolution_subtract_fusion.1.corner_ref), custom_call_target="tpu_custom_call" | custom-call | flops 1966080000 | bytes 2097152 | tf_op jit(solution)/shard_map/pallas_call | solution.py:84
  103.0 4.2 %reshape.106 = f32[4,2,320,2,128]{4,3,2,1,0:T(2,128)} reshape(f32[2560,256]{1,0:T(8,128)} %all-gather.25.cloned.1.call-done) | data formatting | bytes 5242880 | tf_op jit(solution)/shard_map/reshape | solution.py:146
  107.2 3.4 copy.26
  119.8 5.1 %fusion.12 = f32[640,512]{1,0:T(8,128)} fusion(f32[640,512]{0,1:T(8,128)} %copy-done.7, f32[640,512]{0,1:T(8,128)S(1)} %fusion.23), kind=kOutput, calls=%fused_computation.20 | convolution fusion | flops 2014445568 | bytes 6553600 | tf_op jit(solution)/shard_map/dot_general | solution.py:17
  124.9 4.3 %collective-permute-start.1 = (f32[640,512]{1,0:T(8,128)}, f32[640,512]{1,0:T(8,128)}, u32[]{:S(2)}, u32[]{:S(2)}) collective-permute-start(f32[640,512]{1,0:T(8,128)} %fusion.12), channel_id=1, source_target_pairs={{0,8},{8,16},{16,24},{1,9},{9,17},{17,25},{2,10},{10,18},{18,26},{... | collective-permute-start | bytes 3932168 | tf_op jit(solution)/shard_map/ppermute | solution.py:170
  129.3 3.5 fusion.53
  134.1 4.8 %fusion.55 = f32[1024,512]{1,0:T(8,128)} fusion(f32[1024,512]{0,1:T(8,128)S(1)} %fusion.53, f32[512,512]{1,0:T(8,128)S(1)} %copy-done.2), kind=kOutput, calls=%fused_computation.72 | convolution fusion | flops 1610612736 | bytes 5242880 | tf_op jit(solution)/shard_map/dot_general | solution.py:17
  139.0 4.2 %fusion.20 = f32[1024,512]{0,1:T(8,128)S(1)} fusion(f32[512,512]{1,0:T(8,128)S(1)} %shard_map.67, f32[1024,512]{1,0:T(8,128)} %all-gather.15.cloned.1.call-done, f32[1024,512]{1,0:T(8,128)} %fusion.55, pred[1024]{0:T(1024)(128)(4,1)S(1)} %iota_compare_fusion), kind=kOutput, calls=%fused_computation.27 | convolution fusion | flops 1611661312 | bytes 7341056 | tf_op jit(solution)/shard_map/dot_general | solution.py:17
  147.1 5.5 %copy.13 = f32[1,1024,1024]{2,1,0:T(8,128)} copy(f32[1,1024,1024]{1,2,0:T(8,128)} %fusion.10) | data formatting | bytes 8388608
  152.6 4.6 %fusion.29 = f32[640,512]{1,0:T(8,128)S(1)} fusion(s32[]{:T(128)S(6)} %select_n.45, f32[1024,512]{0,1:T(8,128)} %copy-done.4, f32[1024,512]{0,1:T(8,128)} %copy-done.8, f32[640,512]{0,1:T(8,128)} %copy-done.7, f32[640,512]{0,1:T(8,128)S(1)} %fusion.23, f32[1,640,512]{2,1,0:T(8,128)} %param.8), kind=kOutput, calls=%fused_computation.39 | convolution fusion | flops 2014773248 | bytes 9437188 | tf_op jit(solution)/shard_map/dot_general | solution.py:17
  159.3 14.5 %all-reduce.2.cloned.1.call-done = f32[128,128]{1,0:T(8,128)} async-done(((f32[128,128]{1,0:T(8,128)}), f32[128,128]{1,0:T(8,128)}) %all-reduce.2.cloned.1.call-update) | async-done | bytes 65552 | tf_op jit(solution)/shard_map/psum | solution.py:171
  178.2 78.1 %all-gather.21.cloned.1.call-done = f32[1,512,2048]{2,1,0:T(8,128)} async-done(((f32[1,128,2048]{2,1,0:T(8,128)}), f32[1,512,2048]{2,1,0:T(8,128)}) %all-gather.21.cloned.1.call-update) | async-done | bytes 4194320 | tf_op jit(solution)/shard_map/all_gather | solution.py:136
  256.3 5.4 %fusion.5 = f32[512,2048]{1,0:T(8,128)S(1)} fusion(f32[512,512]{1,0:T(8,128)S(1)} %shard_map.66, f32[1,512,2048]{2,1,0:T(8,128)} %all-gather.21.cloned.1.call-done), kind=kOutput, calls=%fused_computation.9 | convolution fusion | flops 3221225472 | bytes 9437184 | tf_op jit(solution)/shard_map/dot_general | solution.py:17
  263.6 5.2 %fusion.56 = f32[512,2048]{1,0:T(8,128)} fusion(f32[512,512]{1,0:T(8,128)S(1)} %copy-done.3, f32[512,2048]{1,0:T(8,128)S(1)} %fusion.5), kind=kOutput, calls=%fused_computation.73 | convolution fusion | flops 3221225472 | bytes 9437184 | tf_op jit(solution)/shard_map/dot_general | solution.py:17
  268.8 68.4 %all-gather.23.cloned.1.call-done = f32[1,512,2048]{2,1,0:T(8,128)} async-done(((f32[1,128,2048]{2,1,0:T(8,128)}), f32[1,512,2048]{2,1,0:T(8,128)}) %all-gather.23.cloned.1.call-update) | async-done | bytes 4194320 | tf_op jit(solution)/shard_map/all_gather | solution.py:136
  337.2 9.0 %fusion.11 = f32[512,2048]{1,0:T(8,128)} fusion(f32[512,512]{1,0:T(8,128)S(1)} %shard_map.67, f32[512,2048]{1,0:T(8,128)} %fusion.56, f32[1,512,2048]{2,1,0:T(8,128)} %all-gather.23.cloned.1.call-done, pred[2048]{0:T(1024)(128)(4,1)S(1)} %fusion.38), kind=kOutput, calls=%fused_computation.18 | convolution fusion | flops 3223322624 | bytes 13633536 | tf_op jit(solution)/shard_map/dot_general | solution.py:17
  346.3 17.4 %fusion.7 = f32[1024,2048]{1,0:T(8,128)} fusion(f32[512,2048]{1,0:T(8,128)} %fusion.11, f32[512,2048]{1,0:T(8,128)S(1)} %copy-done.11, f32[1024,512]{0,1:T(8,128)S(1)} %copy-done.9, f32[1024,512]{0,1:T(8,128)S(1)} %copy-done.6, f32[1,1024,2048]{2,1,0:T(8,128)} %param.7), kind=kOutput, calls=%fused_computation.16 | convolution fusion | flops 12890144768 | bytes 29360128 | tf_op jit(solution)/shard_map/dot_general | solution.py:17
  363.6 3.5 copy.28
  368.8 3.4 copy-done.13
  (86 shorter events, 44.7 us)
Async XLA Ops:
  7.2 29.1 %all-gather.17.cloned.1.call-start = ((), (), s32[]{:S(2)}) async-start(), calls=%async_computation.3 | async-start | bytes 1179648 | tf_op jit(solution)/shard_map/all_gather | solution.py:127
  10.5 1.6 copy-start.14
  11.3 56.1 %all-gather.19.cloned.1.call-start = ((), (), s32[]{:S(2)}) async-start(), calls=%async_computation.4 | async-start | bytes 2359296 | tf_op jit(solution)/shard_map/all_gather | solution.py:127
  12.1 90.9 %all-gather.25.cloned.1.call-start = ((), (), s32[]{:S(2)}) async-start(), calls=%async_computation.7 | async-start | bytes 2949120 | tf_op jit(solution)/shard_map/all_gather | solution.py:145
  12.2 3.6 collective-permute-start
  16.6 112.7 %all-gather.13.cloned.1.call-start = ((), (), s32[]{:S(2)}) async-start(), calls=%async_computation | async-start | bytes 3145728 | tf_op jit(solution)/shard_map/all_gather | solution.py:133
  19.4 119.6 %all-gather.15.cloned.1.call-start = ((), (), s32[]{:S(2)}) async-start(), calls=%async_computation.1 | async-start | bytes 3145728 | tf_op jit(solution)/shard_map/all_gather | solution.py:133
  20.5 153.3 %all-reduce.2.cloned.1.call-start = ((), (), s32[]{:S(2)}) async-start(), calls=%async_computation.2 | async-start | bytes 131072 | tf_op jit(solution)/shard_map/psum | solution.py:171
  110.8 1.4 copy-start.1
  118.3 137.9 %all-gather.21.cloned.1.call-start = ((), (), s32[]{:S(2)}) async-start(), calls=%async_computation.5 | async-start | bytes 5242880 | tf_op jit(solution)/shard_map/all_gather | solution.py:136
  119.1 218.2 %all-gather.23.cloned.1.call-start = ((), (), s32[]{:S(2)}) async-start(), calls=%async_computation.6 | async-start | bytes 5242880 | tf_op jit(solution)/shard_map/all_gather | solution.py:136
  124.9 50.4 %collective-permute-start.1 = (f32[640,512]{1,0:T(8,128)}, f32[640,512]{1,0:T(8,128)}, u32[]{:S(2)}, u32[]{:S(2)}) collective-permute-start(f32[640,512]{1,0:T(8,128)} %fusion.12), channel_id=1, source_target_pairs={{0,8},{8,16},{16,24},{1,9},{9,17},{17,25},{2,10},{10,18},{18,26},{... | collective-permute-start | bytes 3932168 | tf_op jit(solution)/shard_map/ppermute | solution.py:170
  129.3 4.9 %copy-start.2 = (f32[512,512]{1,0:T(8,128)S(1)}, f32[512,512]{1,0:T(8,128)}, u32[]{:S(2)}) copy-start(f32[512,512]{1,0:T(8,128)} %copy-done) | copy-start | bytes 3145732
  132.8 1.3 copy-start.4
  139.0 5.6 %copy-start.5 = (f32[1024,512]{0,1:T(8,128)S(1)}, f32[1024,512]{0,1:T(8,128)}, u32[]{:S(2)}) copy-start(f32[1024,512]{0,1:T(8,128)} %copy-done.4) | copy-start | bytes 6291460
  143.2 1.4 copy-start.8
  157.2 16.6 %copy-start.17 = (f32[128,128]{1,0:T(8,128)S(1)}, f32[128,128]{1,0:T(8,128)}, u32[]{:S(2)}) copy-start(f32[128,128]{1,0:T(8,128)} %param.9) | copy-start | bytes 196612
  178.2 85.4 %copy-start.3 = (f32[512,512]{1,0:T(8,128)S(1)}, f32[512,512]{1,0:T(8,128)}, u32[]{:S(2)}) copy-start(f32[512,512]{1,0:T(8,128)} %copy-done) | copy-start | bytes 3145732
  261.6 2.0 copy-start.10
  337.2 9.0 %copy-start.6 = (f32[1024,512]{0,1:T(8,128)S(1)}, f32[1024,512]{0,1:T(8,128)}, u32[]{:S(2)}) copy-start(f32[1024,512]{0,1:T(8,128)} %copy-done.4) | copy-start | bytes 6291460
  337.2 9.0 %copy-start.9 = (f32[1024,512]{0,1:T(8,128)S(1)}, f32[1024,512]{0,1:T(8,128)}, u32[]{:S(2)}) copy-start(f32[1024,512]{0,1:T(8,128)} %copy-done.8) | copy-start | bytes 6291460
  337.2 9.0 %copy-start.11 = (f32[512,2048]{1,0:T(8,128)S(1)}, f32[512,2048]{1,0:T(8,128)}, u32[]{:S(2)}) copy-start(f32[512,2048]{1,0:T(8,128)} %copy-done.10) | copy-start | bytes 12582916
  363.6 3.7 copy-start.16
  368.8 3.4 copy-start.13
  (4 other events, 4.2 us)
Sparse Core Ops, SparseCore 0:
  11.4 24.7 all-gather.16
  38.4 28.9 all-gather.18
  69.6 33.3 all-gather.24
  104.4 9.5 all-gather.12
  115.9 11.7 all-gather.14
  131.0 42.7 all-reduce.1
  175.5 80.7 all-gather.20
  257.9 79.2 all-gather.22
